TPU v7x, 32 devices: a whole 2x2x4 slice. The times are simulated.
32 devices in a mesh: row: 8 (over z, core), col: 2 (over y), lrn: 2 (over x).
Axes of the slice: x: 2, y: 2, z: 4, core: 2. Of those that a mesh axis runs over, the one named last changes fastest.
Arguments:
- responses: int32 [4096, 16384], P('lrn', ('row', 'col')), may hold values 0 or 1
- observed: int32 [4096, 16384], P('lrn', ('row', 'col')), may hold values from 0 to 1, as said below
- qmatrix: int32 [16384, 8], P(('row', 'col')), may hold values from 0 to 1
- guess: float32 [16384], P(('row', 'col')), may hold values from 0.05 to 0.35
- slip: float32 [16384], P(('row', 'col')), may hold values from 0.05 to 0.35
Outputs:
- q3_scaled: float32 [16384, 16384], P('row', ('col', 'lrn'))
Inputs may be any that keep to these rules, and one draw needn't show every extreme that they name: Some items have no observed response from any learner.
All inputs are finite; a program needn't handle non-finite values. No bound on the sum of `responses` on one device may be relied on, other than what follows from the above.
Results may differ from a plain program's by a relative error of at most 0.008.
Values may be sent and summed in bfloat16 or wider, within the bound.
A program may use at most 192 MiB of HBM per device.

v0:
```python
import jax
import jax.numpy as jnp
from jax import lax
from jax.sharding import PartitionSpec as P

ATTRS = 8
PROFILES = 256


def spread(x, axis, root):
    mine = lax.axis_index(axis) == root
    return lax.psum(jnp.where(mine, x, jnp.zeros_like(x)), axis)


def success(qmatrix, guess, slip):
    codes = jnp.arange(PROFILES, dtype=jnp.int32)
    powers = jnp.arange(ATTRS, dtype=jnp.int32)
    bits = (codes[None, :] >> powers[:, None] & 1).astype(jnp.float32)
    lacking = jnp.dot(qmatrix.astype(jnp.float32), 1.0 - bits, precision=lax.Precision.HIGHEST)
    return jnp.where(lacking == 0.0, 1.0 - slip[:, None], guess[:, None])


def learner_product(left, right):
    return lax.dot_general(
        left, right, (((0,), (0,)), ((), ())), preferred_element_type=jnp.float32
    )


def shards(responses, observed, qmatrix, guess, slip):
    prob = success(qmatrix, guess, slip)
    answered = responses.astype(jnp.float32)
    seen = observed.astype(jnp.float32)
    partial_value = jnp.dot(seen * answered, jnp.log(prob), precision=lax.Precision.HIGHEST)
    partial_value = partial_value + jnp.dot(
        seen * (1.0 - answered), jnp.log(1.0 - prob), precision=lax.Precision.HIGHEST
    )
    loglik = lax.psum(partial_value, ("row", "col"))
    posterior = jax.nn.softmax(loglik, axis=1).astype(jnp.bfloat16)
    expected = jnp.dot(posterior, prob.astype(jnp.bfloat16).T, preferred_element_type=jnp.float32)
    resid = seen * (answered - expected)
    count, total, square = lax.psum(
        (jnp.sum(seen, axis=0), jnp.sum(resid, axis=0), jnp.sum(resid * resid, axis=0)), "lrn"
    )
    count = jnp.maximum(count, 1.0)
    mean = total / count
    var = square / count - mean * mean
    zres = (seen * (resid - mean) * lax.rsqrt(var + 1e-06) * lax.rsqrt(count)).astype(jnp.bfloat16)
    panel = lax.all_gather(zres, "col", axis=1, tiled=True)
    learner_total = zres.shape[0] * lax.axis_size("lrn")
    whole_panel = lax.all_gather(panel, "lrn", axis=0, tiled=True)
    repeats = lax.axis_size("row") // (lax.axis_size("col") * lax.axis_size("lrn"))
    tile_index = lax.axis_index("col") * lax.axis_size("lrn") + lax.axis_index("lrn")
    pieces = [
        spread(whole_panel, "row", tile_index * repeats + offset) for offset in range(repeats)
    ]
    columns = jnp.concatenate(pieces, axis=1)
    gram = learner_product(whole_panel, columns)
    return gram * jnp.sqrt(jnp.float32(learner_total))


def solution(mesh):
    placed = (
        P("lrn", ("row", "col")),
        P("lrn", ("row", "col")),
        P(("row", "col"), None),
        P(("row", "col")),
        P(("row", "col")),
    )
    return jax.shard_map(
        shards, mesh=mesh, in_specs=placed, out_specs=P("row", ("col", "lrn")), check_vma=False
    )
```

profile of v0, /device:TPU:6, one launch (start us, length us, event | category | flops | bytes accessed | tf_op | source)
XLA Modules:
  0.0 1225.6 jit_solution(12633112571260260623)
XLA Ops:
  6.5 0.0 all-reduce.5.cloned.1.call-start
  6.5 0.7 broadcast_subtract_fusion
  7.2 0.0 slice-start
  7.2 1.9 fusion.20
  9.2 0.0 copy-start.1
  9.2 0.0 slice-start.1
  9.2 0.0 copy-start
  9.2 11.8 fusion.7
  21.0 0.0 copy-done.1
  21.1 0.0 slice-done
  21.1 0.0 slice-done.1
  21.1 0.0 copy-done
  21.1 8.7 fusion.17
  29.8 0.0 all-reduce.5.cloned.1.call-update
  29.8 0.2 all-gather.3.cloned.1.call-start
  30.1 98.8 %all-reduce.5.cloned.1.call-done = f32[2048,256]{1,0:T(8,128)} async-done(((f32[2048,256]{1,0:T(8,128)}), f32[2048,256]{1,0:T(8,128)}) %all-reduce.5.cloned.1.call-update) | async-done | bytes 2097168 | tf_op jit(solution)/shard_map/psum | solution.py:37
  128.9 6.2 online-softmax
  135.1 13.4 %fusion.38 = (f32[1024]{0:T(1024)S(1)}, f32[1024]{0:T(1024)S(1)}, f32[2048,1024]{1,0:T(8,128)}, f32[1024]{0:T(1024)S(1)}) fusion(f32[2048,1024]{1,0:T(8,128)} %online-softmax, s32[2048,1024]{1,0:T(8,128)} %param.5, s32[2048,1024]{1,0:T(8,128)} %param.6), kind=kLoop, calls=%fused_computation.45 | loop fusion | flops 16774144 | bytes 33566720 | tf_op jit(solution)/shard_map/reduce_sum | solution.py:42
  148.5 7.1 all-reduce
  155.6 10.1 multiply_convert_fusion
  165.7 0.0 all-gather.3.cloned.1.call-update
  165.7 0.0 all-gather.5.cloned.1.call-start
  165.8 102.6 %all-gather.3.cloned.1.call-done = bf16[2048,2048]{1,0:T(8,128)(2,1)} async-done(((bf16[2048,1024]{1,0:T(8,128)(2,1)}), bf16[2048,2048]{1,0:T(8,128)(2,1)}) %all-gather.3.cloned.1.call-update) | async-done | bytes 8388624 | tf_op jit(solution)/shard_map/all_gather | solution.py:48
  268.4 0.0 all-gather.5.cloned.1.call-update
  268.4 0.0 all-reduce.7.cloned.1.call-start
  268.5 200.4 %all-gather.5.cloned.1.call-done = bf16[4096,2048]{1,0:T(8,128)(2,1)} async-done(((bf16[2048,2048]{1,0:T(8,128)(2,1)}), bf16[4096,2048]{1,0:T(8,128)(2,1)}) %all-gather.5.cloned.1.call-update) | async-done | bytes 16777232 | tf_op jit(solution)/shard_map/all_gather | solution.py:50
  468.9 18.3 %broadcast_select_fusion.1 = (bf16[4096,2048]{1,0:T(8,128)(2,1)}, bf16[4096,2048]{1,0:T(8,128)(2,1)}) fusion(bf16[4096,2048]{1,0:T(8,128)(2,1)} %all-gather.5.cloned.1.call-done, pred[]{:T(512)S(6)} %eq.15, pred[]{:T(512)S(6)} %eq.16), kind=kLoop, calls=%fused_computation.6 | loop fusion | flops 16777216 | bytes 50331648 | tf_op jit(solution)/shard_map/jit(_where)/select_n | solution.py:12
  487.2 0.0 all-reduce.7.cloned.1.call-update
  487.2 650.7 %all-reduce.7.cloned.1.call-done = (bf16[4096,2048]{1,0:T(8,128)(2,1)}, bf16[4096,2048]{1,0:T(8,128)(2,1)}) async-done(((bf16[4096,2048]{1,0:T(8,128)(2,1)}, bf16[4096,2048]{1,0:T(8,128)(2,1)}), (bf16[4096,2048]{1,0:T(8,128)(2,1)}, bf16[4096,2048]{1,0:T(8,128)(2,1)})) %all-reduce.7.cloned.1.call-update) | async-done | bytes 33554448 | tf_op jit(solution)/shard_map/psum | solution.py:12
  1137.9 81.1 %fusion.4 = f32[2048,4096]{1,0:T(8,128)} fusion(bf16[4096,2048]{1,0:T(8,128)(2,1)} %all-gather.5.cloned.1.call-done, bf16[4096,2048]{1,0:T(8,128)(2,1)} %get-tuple-element.10, bf16[4096,2048]{1,0:T(8,128)(2,1)} %get-tuple-element.11), kind=kOutput, calls=%fused_computation.4 | convolution fusion | flops 68794974208 | bytes 83886080 | tf_op jit(solution)/shard_map/dot_general | solution.py:24
  (2 shorter events, 0.0 us)
Async XLA Ops:
  6.5 122.4 %all-reduce.5.cloned.1.call-start = ((), (), s32[]{:S(2)}) async-start(), calls=%async_computation | async-start | bytes 4194304 | tf_op jit(solution)/shard_map/psum | solution.py:37
  7.2 13.8 %slice-start = ((s8[8388608]{0:T(1024)(128)(4,1)}), s8[4194304]{0:T(1024)(128)(4,1)S(1)}, s32[]{:S(2)}) async-start(s8[8388608]{0:T(1024)(128)(4,1)} %bitcast.2), calls=%async_computation.4 | async-start | bytes 8388608
  9.2 11.9 copy-start.1
  9.2 11.9 slice-start.1
  9.2 11.9 copy-start
  29.8 238.5 %all-gather.3.cloned.1.call-start = ((), (), s32[]{:S(2)}) async-start(), calls=%async_computation.1 | async-start | bytes 12582912 | tf_op jit(solution)/shard_map/all_gather | solution.py:48
  165.7 303.2 %all-gather.5.cloned.1.call-start = ((), (), s32[]{:S(2)}) async-start(), calls=%async_computation.2 | async-start | bytes 25165824 | tf_op jit(solution)/shard_map/all_gather | solution.py:50
  268.4 869.5 %all-reduce.7.cloned.1.call-start = ((), (), s32[]{:S(2)}) async-start(), calls=%async_computation.3 | async-start | bytes 67108864 | tf_op jit(solution)/shard_map/psum | solution.py:12
Sparse Core Ops, SparseCore 0:
  30.0 98.9 all-reduce.4
  165.8 102.4 all-gather.2
  270.0 198.8 all-gather.4
  487.3 650.5 all-reduce.6
where the time goes:
time: 1230 us
  waiting for transfers between devices  1050 us (85%)
  matrix products  104 us (8%)
  other arithmetic  42.4 us (3%)
  between operations  13.2 us (1%)
    psum x1, waiting for transfers between devices, spread(): return lax.psum(jnp.where(mine, x, jnp.zeros_like(x)), axis)  651 us
    all_gather x1, waiting for transfers between devices, shards(): whole_panel = lax.all_gather(panel, 'lrn', axis=0, tiled=True)  200 us
    all_gather x1, waiting for transfers between devices, shards(): panel = lax.all_gather(zres, 'col', axis=1, tiled=True)  103 us
    psum x1, waiting for transfers between devices, shards(): loglik = lax.psum(partial_value, ('row', 'col'))  98.8 us
    dot_general x1, matrix products, learner_product(): lax.dot_general(left, right, (((0,), (0,)), ((), ())), preferred_element_...  81.1 us
  transfers between devices with their start and end apart: 4, of which 4 were waited for; matrix products, arithmetic and copies ran while one was open for 0% of the time, Pallas kernels for 0%

commit v1 on v0

v1 whole, which is shorter than its diff:
```python
import functools

import jax
import jax.numpy as jnp
from jax import lax
from jax.experimental import pallas as pl
from jax.experimental.pallas import tpu as pltpu
from jax.sharding import PartitionSpec as P

ATTRS = 8
PROFILES = 256
CHUNK = 128
GROUP = 2 * CHUNK
TILE = 512
AHEAD = 3
MESH = pl.DeviceIdType.MESH


def spread(x, axis, root):
    mine = lax.axis_index(axis) == root
    return lax.psum(jnp.where(mine, x, jnp.zeros_like(x)), axis)


def mastered(qmatrix):
    codes = jnp.arange(PROFILES, dtype=jnp.int32)
    powers = jnp.arange(ATTRS, dtype=jnp.int32)
    bits = (codes[None, :] >> powers[:, None] & 1).astype(jnp.float32)
    lacking = jnp.dot(qmatrix.astype(jnp.float32), 1.0 - bits, precision=lax.Precision.HIGHEST)
    return lacking == 0.0


def learner_product(left, right):
    return lax.dot_general(
        left, right, (((0,), (0,)), ((), ())), preferred_element_type=jnp.float32
    )


def head(x):
    return lax.reduce_precision(x, 8, 7)


def residuals(responses, observed, qmatrix, guess, slip):
    full = mastered(qmatrix)
    prob = jnp.where(full, 1.0 - slip[:, None], guess[:, None])
    answered = responses.astype(jnp.float32)
    seen = observed.astype(jnp.float32)
    high = 1.0 - slip
    right = jnp.log(high) - jnp.log(guess)
    wrong = jnp.log(1.0 - high) - jnp.log(1.0 - guess)
    gain = seen * (answered * right + (1.0 - answered) * wrong)
    first = head(gain)
    second = head(gain - first)
    third = head(gain - first - second)
    select = full.astype(jnp.bfloat16)
    partial_value = sum(
        jnp.dot(part.astype(jnp.bfloat16), select, preferred_element_type=jnp.float32)
        for part in (third, second, first)
    )
    loglik = lax.psum_scatter(partial_value, ("row", "col"), scatter_dimension=0, tiled=True)
    posterior = jax.nn.softmax(loglik, axis=1).astype(jnp.bfloat16)
    posterior = lax.all_gather(posterior, ("row", "col"), axis=0, tiled=True)
    expected = jnp.dot(posterior, prob.astype(jnp.bfloat16).T, preferred_element_type=jnp.float32)
    resid = seen * (answered - expected)
    count, total, square = lax.psum(
        (jnp.sum(seen, axis=0), jnp.sum(resid, axis=0), jnp.sum(resid * resid, axis=0)), "lrn"
    )
    count = jnp.maximum(count, 1.0)
    mean = total / count
    var = square / count - mean * mean
    return (seen * (resid - mean) * lax.rsqrt(var + 1e-06) * lax.rsqrt(count)).astype(jnp.bfloat16)


def gram_kernel(planes, scale, z_ref, out_ref, panel, cols, stage, own_sem, out_sem,
                xs, xr, ys, yr, us, ds, zr, ss, sr):
    items = z_ref.shape[0]
    n = items // CHUNK
    r, c, l = lax.axis_index("row"), lax.axis_index("col"), lax.axis_index("lrn")
    plane, core = r // 2, r % 2
    line = c * 2 + l
    source = plane == line
    goes_up = (plane >= line) & (plane < planes - 1)
    goes_down = (plane <= line) & (plane > 0)
    x_to, y_to = (r, c, 1 - l), (r, 1 - c, l)
    up_to, down_to, twin = (r + 2, c, l), (r - 2, c, l), (r + 1 - 2 * core, c, l)

    barrier = pltpu.get_barrier_semaphore()
    for other in (x_to, y_to, twin):
        pl.semaphore_signal(barrier, inc=1, device_id=other, device_id_type=MESH)

    @pl.when(plane < planes - 1)
    def _():
        pl.semaphore_signal(barrier, inc=1, device_id=up_to, device_id_type=MESH)

    @pl.when(plane > 0)
    def _():
        pl.semaphore_signal(barrier, inc=1, device_id=down_to, device_id_type=MESH)

    ends = jnp.where(plane == 0, 1, 0) + jnp.where(plane == planes - 1, 1, 0)
    pl.semaphore_wait(barrier, 5 - ends)

    own = pltpu.make_async_copy(z_ref, panel.at[l, c], own_sem)
    own.start()
    own.wait()

    def rows(i):
        return pl.ds(pl.multiple_of(i * CHUNK, CHUNK), CHUNK)

    def remote(src, dst, send, recv, to):
        return pltpu.make_async_remote_copy(
            src_ref=src, dst_ref=dst, send_sem=send, recv_sem=recv,
            device_id=to, device_id_type=MESH,
        )

    def x_copy(far, i):
        ref = panel.at[l, (1 - c) if far else c, rows(i)]
        at = i + n * far
        return remote(ref, ref, xs.at[at], xr.at[at], x_to)

    def x_wait(far, i):
        ref = panel.at[1 - l, (1 - c) if far else c, rows(i)]
        at = i + n * far
        remote(ref, ref, xs.at[at], xr.at[at], x_to).wait_recv()

    def y_copy(i):
        ref = panel.at[l, c, rows(i)]
        return remote(ref, ref, ys.at[i], yr.at[i], y_to)

    def y_wait(i):
        ref = panel.at[l, 1 - c, rows(i)]
        remote(ref, ref, ys.at[i], yr.at[i], y_to).wait_recv()

    def place(q):
        far, i, cross = q // (2 * n), (q % (2 * n)) // 2, q % 2
        return l + cross - 2 * l * cross, c + far - 2 * c * far, i

    def chunk(which, q):
        px, py, i = place(q)
        return cols.at[which, px, py, rows(i)]

    def up_copy(q):
        return remote(chunk(core, q), chunk(core, q), us.at[q], zr.at[q], up_to)

    def down_copy(q):
        return remote(chunk(core, q), chunk(core, q), ds.at[q], zr.at[q], down_to)

    def twin_copy(q):
        return remote(chunk(core, q), chunk(core, q), ss.at[q], sr.at[q], twin)

    def sent(q):
        @pl.when(goes_up)
        def _():
            up_copy(q).wait_send()

        @pl.when(goes_down)
        def _():
            down_copy(q).wait_send()

        twin_copy(q).wait_send()

    def relay(q):
        @pl.when(source)
        def _():
            px, py, i = place(q)
            move = pltpu.make_async_copy(panel.at[px, py, rows(i)], chunk(core, q), own_sem)
            move.start()
            move.wait()

        @pl.when(jnp.logical_not(source))
        def _():
            up_copy(q).wait_recv()

        @pl.when(q >= AHEAD)
        def _():
            sent(q - AHEAD)

        @pl.when(goes_up)
        def _():
            up_copy(q).start()

        @pl.when(goes_down)
        def _():
            down_copy(q).start()

        twin_copy(q).start()

    def out_copy(slot, start):
        return pltpu.make_async_copy(
            stage.at[slot], out_ref.at[:, pl.ds(pl.multiple_of(start, GROUP), GROUP)],
            out_sem.at[slot],
        )

    def job(j):
        g, swap, slot = j // 2, j % 2, j % 2
        which = core + swap - 2 * core * swap

        @pl.when(swap == 1)
        def _():
            for s in range(4):
                q = 4 * g + s
                remote(chunk(which, q), chunk(which, q), ss.at[q], sr.at[q], twin).wait_recv()

        far = g // (n // 2)
        py = c + far - 2 * c * far
        base = pl.multiple_of((g % (n // 2)) * GROUP, GROUP)

        @pl.when(j >= 2)
        def _():
            out_copy(slot, 0).wait()

        per = items // TILE

        @pl.loop(0, 2 * per)
        def _(m):
            y2, off = m // per, pl.multiple_of((m % per) * TILE, TILE)
            acc = None
            for px in range(2):
                term = lax.dot_general(
                    panel[px, y2, pl.ds(off, TILE), :],
                    cols[which, px, py, pl.ds(base, GROUP), :],
                    (((1,), (1,)), ((), ())), preferred_element_type=jnp.float32,
                )
                acc = term if acc is None else acc + term
            stage[slot, pl.ds(pl.multiple_of(m * TILE, TILE), TILE), :] = acc * scale

        out_copy(slot, which * 2 * items + py * items + base).start()

    @pl.loop(0, 2 * n)
    def _(q):
        @pl.when(q < n)
        def _():
            x_copy(0, q).start()
            y_copy(q).start()

        @pl.when(q >= n)
        def _():
            y_wait(q - n)
            x_copy(1, q - n).start()

        @pl.when(q % 2 == 1)
        def _():
            x_wait(0, q // 2)

        relay(q)

    @pl.loop(0, n)
    def _(i):
        x_wait(1, i)

    @pl.loop(2 * n, 4 * n)
    def _(q):
        relay(q)

        @pl.when(q > 2 * n)
        def _():
            job(q - 2 * n - 1)

    job(2 * n - 1)

    @pl.loop(4 * n - AHEAD, 4 * n)
    def _(q):
        sent(q)

    @pl.loop(0, n)
    def _(i):
        x_copy(0, i).wait_send()
        x_copy(1, i).wait_send()
        y_copy(i).wait_send()

    out_copy(0, 0).wait()
    out_copy(1, 0).wait()


def line_gram(planes, scale, z):
    items, half = z.shape
    n = items // CHUNK
    dma = pltpu.SemaphoreType.DMA
    return pl.pallas_call(
        functools.partial(gram_kernel, planes, scale),
        out_shape=jax.ShapeDtypeStruct((2 * items, 4 * items), jnp.float32),
        in_specs=[pl.BlockSpec(memory_space=pl.ANY)],
        out_specs=pl.BlockSpec(memory_space=pl.ANY),
        scratch_shapes=[
            pltpu.VMEM((2, 2, items, half), jnp.bfloat16),
            pltpu.VMEM((2, 2, 2, items, half), jnp.bfloat16),
            pltpu.VMEM((2, 2 * items, GROUP), jnp.float32),
            dma, dma((2,)),
            dma((2 * n,)), dma((2 * n,)), dma((n,)), dma((n,)),
            dma((4 * n,)), dma((4 * n,)), dma((4 * n,)), dma((4 * n,)), dma((4 * n,)),
        ],
        compiler_params=pltpu.CompilerParams(
            collective_id=0, has_side_effects=True, vmem_limit_bytes=60 * 2**20
        ),
        cost_estimate=pl.CostEstimate(
            flops=2 * 2 * items * 4 * items * 2 * half,
            bytes_accessed=4 * 8 * items * items, transcendentals=0,
        ),
    )(z)


def shards(responses, observed, qmatrix, guess, slip):
    zres = residuals(responses, observed, qmatrix, guess, slip)
    learner_total = zres.shape[0] * lax.axis_size("lrn")
    tiles = lax.axis_size("col") * lax.axis_size("lrn")
    repeats = lax.axis_size("row") // tiles
    if lax.axis_size("col") == 2 and lax.axis_size("lrn") == 2 and repeats == 2:
        return line_gram(tiles, float(learner_total) ** 0.5, zres.T)
    panel = lax.all_gather(zres, "col", axis=1, tiled=True)
    whole_panel = lax.all_gather(panel, "lrn", axis=0, tiled=True)
    tile_index = lax.axis_index("col") * lax.axis_size("lrn") + lax.axis_index("lrn")
    pieces = [
        spread(whole_panel, "row", tile_index * repeats + offset) for offset in range(repeats)
    ]
    columns = jnp.concatenate(pieces, axis=1)
    gram = learner_product(whole_panel, columns)
    return gram * jnp.sqrt(jnp.float32(learner_total))


def solution(mesh):
    placed = (
        P("lrn", ("row", "col")),
        P("lrn", ("row", "col")),
        P(("row", "col"), None),
        P(("row", "col")),
        P(("row", "col")),
    )
    return jax.shard_map(
        shards, mesh=mesh, in_specs=placed, out_specs=P("row", ("col", "lrn")), check_vma=False
    )
```

time: 1230 us -> 602 us (0.49)
  waiting for transfers between devices: 1050 us -> 99 us
  Pallas kernels: 6.19 us -> 400 us
  matrix products: 104 us -> 17.8 us
  local copies, waits for them, and re-layouts: 0.02 us -> 41.3 us
  other arithmetic: 42.4 us -> 20 us
    psum x2 -> x0, waiting for transfers between devices: 750 us -> none  [the longest x1 651 us: spread(): return lax.psum(jnp.where(mine, x, jnp.zeros_like(x)), axis)]
    pallas_call x0 -> x1, Pallas kernels: none -> 400 us  [line_gram(): pl.pallas_call(functools.partial(gram_kernel, planes, scale), out_shape=j...]
    all_gather x2 -> x1, waiting for transfers between devices: 303 us -> 36.5 us  [residuals(): posterior = lax.all_gather(posterior, ('row', 'col'), axis=0, tiled=True)]
    dot_general x4 -> x5, matrix products: 104 us -> 17.8 us  [the longest x1 9.87 us: residuals(): jnp.dot(posterior, prob.astype(jnp.bfloat16).T, preferred_element_type=jn...]
    reduce_scatter x0 -> x1, waiting for transfers between devices: none -> 62.5 us  [residuals(): lax.psum_scatter(partial_value, ('row', 'col'), scatter_dimension=0, tile...]
    unnamed x8 -> x7, local copies, waits for them, and re-layouts: 0.02 us -> 41.3 us
    select_n x1 -> x0, other arithmetic: 18.3 us -> none  [spread(): return lax.psum(jnp.where(mine, x, jnp.zeros_like(x)), axis)]
  transfers between devices with their start and end apart: 4 -> 2, of which waited for: 4 -> 2; matrix products, arithmetic and copies ran while one was open for 0% -> 0% of each run, Pallas kernels for 0% -> 0%
where the time goes in v1:
time: 602 us; the launch traced here: 599 us
  Pallas kernels  400 us (66%)
  waiting for transfers between devices  99 us (16%)
  local copies, waits for them, and re-layouts  41.3 us (7%)
  other arithmetic  20 us (3%)
  matrix products  17.8 us (3%)
  between operations  13.5 us (2%)
  blocking collectives  7.11 us (1%)
    pallas_call x1, Pallas kernels, line_gram(): pl.pallas_call(functools.partial(gram_kernel, planes, scale), out_shape=j...  400 us
    reduce_scatter x1, waiting for transfers between devices, residuals(): lax.psum_scatter(partial_value, ('row', 'col'), scatter_dimension=0, tile...  62.5 us
    unnamed x7, local copies, waits for them, and re-layouts  41.3 us
    all_gather x1, waiting for transfers between devices, residuals(): posterior = lax.all_gather(posterior, ('row', 'col'), axis=0, tiled=True)  36.5 us
  transfers between devices with their start and end apart: 2, of which 2 were waited for; matrix products, arithmetic and copies ran while one was open for 0% of the time, Pallas kernels for 0%

profile of v1, /device:TPU:6, one launch (start us, length us, event | category | flops | bytes accessed | tf_op | source)
XLA Modules:
  0.0 599.2 jit_solution(4880506266236997635)
XLA Ops:
  6.5 0.0 reduce-scatter.2.cloned.1.call-start
  6.5 1.8 convolution_compare_fusion
  8.4 9.1 %copy.6 = s32[2048,1024]{0,1:T(8,128)} copy(s32[2048,1024]{1,0:T(8,128)} %param.6) | data formatting | bytes 16777216 | tf_op args[1]
  17.5 0.0 copy-start
  17.5 0.0 copy-start.1
  17.5 9.2 %copy.7 = s32[2048,1024]{0,1:T(8,128)} copy(s32[2048,1024]{1,0:T(8,128)} %param.5) | data formatting | bytes 16777216 | tf_op args[0]
  26.7 0.0 copy-done
  26.7 0.0 copy-done.1
  26.7 7.3 %convert_reduce_fusion = (f32[1024]{0:T(1024)S(1)}, f32[2048,1024]{0,1:T(8,128)S(1)}) fusion(s32[2048,1024]{0,1:T(8,128)} %copy.6, f32[1024]{0:T(1024)S(1)} %get-tuple-element.15, f32[1024]{0:T(1024)S(1)} %get-tuple-element.14, s32[2048,1024]{0,1:T(8,128)} %copy.7), kind=kLoop, calls=%fused_computation.10 | loop fusion | flops 16776192 | bytes 25178112 | tf_op jit(solution)/shard_map/reduce_sum | solution.py:65
  34.0 1.4 fusion.4
  35.5 1.8 fusion.7
  37.3 2.8 fusion.10
  40.2 0.0 reduce-scatter.2.cloned.1.call-update
  40.2 0.0 all-gather.2.cloned.1.call-start
  40.2 62.5 %reduce-scatter.2.cloned.1.call-done = f32[128,256]{1,0:T(8,128)} async-done(((f32[2048,256]{1,0:T(8,128)}), f32[128,256]{1,0:T(8,128)}) %reduce-scatter.2.cloned.1.call-update) | async-done | bytes 131088 | tf_op jit(solution)/shard_map/reduce_scatter | solution.py:59
  102.7 1.0 reduce_max.9
  103.7 1.1 fusion.13
  104.8 1.6 divide_convert_fusion
  106.5 0.0 all-gather.2.cloned.1.call-update
  106.5 36.5 %all-gather.2.cloned.1.call-done = bf16[2048,256]{1,0:T(8,128)(2,1)} async-done(((bf16[128,256]{1,0:T(8,128)(2,1)}), bf16[2048,256]{1,0:T(8,128)(2,1)}) %all-gather.2.cloned.1.call-update) | async-done | bytes 1048592 | tf_op jit(solution)/shard_map/all_gather | solution.py:61
  143.0 9.9 %fusion.25 = (f32[1024]{0:T(1024)S(1)}, f32[1024]{0:T(1024)S(1)}, f32[2048,1024]{0,1:T(8,128)}) fusion(bf16[2048,256]{1,0:T(8,128)(2,1)} %all-gather.2.cloned.1.call-done, pred[256,1024]{1,0:T(32,128)(4,1)S(1)} %convolution_compare_fusion, f32[1024]{0:T(1024)S(1)} %copy-done.1, bf16[1024]{0:T(1024)(128)(2,1)S(1)} %broadcast_subtract_fusion, ...), kind=kOutput, calls=%fused_computation.41 | convolution fusion | flops 1088681984 | bytes 26490880 | tf_op jit(solution)/shard_map/dot_general | solution.py:62
  152.9 7.1 %all-reduce = (f32[1024]{0:T(1024)S(1)}, f32[1024]{0:T(1024)S(1)}, f32[1024]{0:T(1024)S(1)}) all-reduce(f32[1024]{0:T(1024)S(1)} %get-tuple-element.10, f32[1024]{0:T(1024)S(1)} %get-tuple-element.6, f32[1024]{0:T(1024)S(1)} %get-tuple-element.5), channel_id=1, replica_groups=mesh['row'=8,'col'=2,'lrn'=2] {'lrn'}, use_global_device_ids=true, to_apply=%region_6.7 | all-reduce | flops 3072 | bytes 24576 | tf_op jit(solution)/shard_map/psum | solution.py:64
  160.0 9.0 %fusion.2.z_ref = bf16[1024,2048]{1,0:T(8,128)(2,1)} fusion(f32[2048,1024]{0,1:T(8,128)} %get-tuple-element.17, s32[2048,1024]{0,1:T(8,128)} %copy.6, f32[1024]{0:T(1024)S(1)} %get-tuple-element.16, f32[1024]{0:T(1024)S(1)} %get-tuple-element.13, f32[1024]{0:T(1024)S(1)} %get-tuple-element.12), kind=kLoop, calls=%fused_computation.11 | loop fusion | flops 12582912 | bytes 20983808 | tf_op jit(solution)/shard_map/transpose | solution.py:306
  168.9 400.4 %shard_map.55 = f32[2048,4096]{1,0:T(8,128)} custom-call(bf16[1024,2048]{1,0:T(8,128)(2,1)} %fusion.2.z_ref), custom_call_target="tpu_custom_call" | custom-call | flops 68719476736 | bytes 33554432 | tf_op jit(solution)/shard_map/pallas_call | solution.py:277
  569.3 23.0 %copy.16 = f32[2048,4096]{1,0:T(8,128)} copy(f32[2048,4096]{1,0:T(8,128)} %shard_map.55) | data formatting | bytes 67108864
  (3 shorter events, 0.0 us)
Async XLA Ops:
  6.5 96.2 %reduce-scatter.2.cloned.1.call-start = ((), (), s32[]{:S(2)}) async-start(), calls=%async_computation.1 | async-start | bytes 2228224 | tf_op jit(solution)/shard_map/reduce_scatter | solution.py:59
  17.5 9.2 %copy-start = (f32[1024]{0:T(1024)S(1)}, f32[1024]{0:T(1024)}, u32[]{:S(2)}) copy-start(f32[1024]{0:T(1024)} %param.9) | copy-start | bytes 12292
  17.5 9.2 %copy-start.1 = (f32[1024]{0:T(1024)S(1)}, f32[1024]{0:T(1024)}, u32[]{:S(2)}) copy-start(f32[1024]{0:T(1024)} %param.8) | copy-start | bytes 12292
  40.2 102.8 %all-gather.2.cloned.1.call-start = ((), (), s32[]{:S(2)}) async-start(), calls=%async_computation.2 | async-start | bytes 1114112 | tf_op jit(solution)/shard_map/all_gather | solution.py:61
Sparse Core Ops, SparseCore 0:
  40.3 62.3 reduce-scatter.1
  106.6 36.3 all-gather.1

commit v2 on v1

--- a/solution.py
+++ b/solution.py
@@ -4,6 +4,7 @@
 import jax.numpy as jnp
 from jax import lax
 from jax.experimental import pallas as pl
+from jax.experimental.layout import Layout, with_layout_constraint
 from jax.experimental.pallas import tpu as pltpu
 from jax.sharding import PartitionSpec as P
 
@@ -37,6 +38,125 @@
 
 def head(x):
     return lax.reduce_precision(x, 8, 7)
+
+
+def compact():
+    sizes = [lax.axis_size(axis) for axis in ("row", "col", "lrn")]
+    return sizes == [8, 2, 2]
+
+
+def posterior_kernel(planes, p_ref, out_ref, from_twin, from_y, from_z, sums,
+                     send, recv, z_send, z_recv, g_send, g_recv):
+    learners = p_ref.shape[0]
+    half, quarter = learners // 2, learners // 4
+    piece = quarter // planes
+    r, c, l = lax.axis_index("row"), lax.axis_index("col"), lax.axis_index("lrn")
+    plane, core = r // 2, r % 2
+    twin, y_to = (r + 1 - 2 * core, c, l), (r, 1 - c, l)
+
+    def z_to(step):
+        there = lax.rem(plane + step, planes)
+        return there, (2 * there + core, c, l)
+
+    barrier = pltpu.get_barrier_semaphore()
+    pl.semaphore_signal(barrier, inc=1, device_id=twin, device_id_type=MESH)
+    pl.semaphore_signal(barrier, inc=1, device_id=y_to, device_id_type=MESH)
+    for step in range(1, planes):
+        pl.semaphore_signal(barrier, inc=1, device_id=z_to(step)[1], device_id_type=MESH)
+    pl.semaphore_wait(barrier, 1 + planes)
+
+    def span(start, size):
+        return pl.ds(pl.multiple_of(start, piece), size)
+
+    def remote(src, dst, send_sem, recv_sem, to):
+        return pltpu.make_async_remote_copy(
+            src_ref=src, dst_ref=dst, send_sem=send_sem, recv_sem=recv_sem,
+            device_id=to, device_id_type=MESH,
+        )
+
+    first = remote(p_ref.at[span((1 - core) * half, half)], from_twin, send.at[0], recv.at[0], twin)
+    first.start()
+    first.wait()
+    sums[...] = p_ref[span(core * half, half), :] + from_twin[...]
+
+    second = remote(sums.at[span((1 - c) * quarter, quarter)], from_y, send.at[1], recv.at[1], y_to)
+    second.start()
+    second.wait()
+    mine = span(c * quarter, quarter)
+    sums[mine, :] = sums[mine, :] + from_y[...]
+
+    thirds = []
+    for step in range(1, planes):
+        there, to = z_to(step)
+        copy = remote(
+            sums.at[span(c * quarter + there * piece, piece)], from_z.at[step - 1],
+            z_send.at[step - 1], z_recv.at[step - 1], to,
+        )
+        copy.start()
+        thirds.append(copy)
+    for copy in thirds:
+        copy.wait()
+    loglik = sums[span(c * quarter + plane * piece, piece), :]
+    for step in range(1, planes):
+        loglik = loglik + from_z[step - 1]
+    weight = jnp.exp(loglik - jnp.max(loglik, axis=1, keepdims=True))
+    weight = weight / jnp.sum(weight, axis=1, keepdims=True)
+    base = core * half + c * quarter
+    own = span(base + plane * piece, piece)
+    out_ref[own, :] = weight.astype(out_ref.dtype)
+
+    copies = []
+    for step in range(1, planes):
+        copy = remote(
+            out_ref.at[own], out_ref.at[own], g_send.at[step - 1], g_recv.at[step - 1],
+            z_to(step)[1],
+        )
+        copy.start()
+        copies.append(copy)
+    for step in range(1, planes):
+        copies[step - 1].wait_send()
+        came = lax.rem(plane + planes - step, planes)
+        block = out_ref.at[span(base + came * piece, piece)]
+        remote(
+            block, block, g_send.at[step - 1], g_recv.at[step - 1], z_to(step)[1]
+        ).wait_recv()
+
+    block = out_ref.at[span(base, quarter)]
+    along = remote(block, block, send.at[2], recv.at[2], y_to)
+    along.start()
+    along.wait_send()
+    block = out_ref.at[span(core * half + (1 - c) * quarter, quarter)]
+    remote(block, block, send.at[2], recv.at[2], y_to).wait_recv()
+
+    block = out_ref.at[span(core * half, half)]
+    across = remote(block, block, send.at[3], recv.at[3], twin)
+    across.start()
+    across.wait_send()
+    block = out_ref.at[span((1 - core) * half, half)]
+    remote(block, block, send.at[3], recv.at[3], twin).wait_recv()
+
+
+def shared_posterior(planes, partial_value):
+    learners, profiles = partial_value.shape
+    dma = pltpu.SemaphoreType.DMA
+    f32 = jnp.float32
+    return pl.pallas_call(
+        functools.partial(posterior_kernel, planes),
+        out_shape=jax.ShapeDtypeStruct((learners, profiles), jnp.bfloat16),
+        in_specs=[pl.BlockSpec(memory_space=pltpu.VMEM)],
+        out_specs=pl.BlockSpec(memory_space=pltpu.VMEM),
+        scratch_shapes=[
+            pltpu.VMEM((learners // 2, profiles), f32),
+            pltpu.VMEM((learners // 4, profiles), f32),
+            pltpu.VMEM((planes - 1, learners // 4 // planes, profiles), f32),
+            pltpu.VMEM((learners // 2, profiles), f32),
+            dma((4,)), dma((4,)),
+            dma((planes - 1,)), dma((planes - 1,)), dma((planes - 1,)), dma((planes - 1,)),
+        ],
+        compiler_params=pltpu.CompilerParams(
+            collective_id=1, has_side_effects=True, vmem_limit_bytes=32 * 2**20
+        ),
+    )(partial_value)
 
 
 def residuals(responses, observed, qmatrix, guess, slip):
@@ -56,9 +176,12 @@
         jnp.dot(part.astype(jnp.bfloat16), select, preferred_element_type=jnp.float32)
         for part in (third, second, first)
     )
-    loglik = lax.psum_scatter(partial_value, ("row", "col"), scatter_dimension=0, tiled=True)
-    posterior = jax.nn.softmax(loglik, axis=1).astype(jnp.bfloat16)
-    posterior = lax.all_gather(posterior, ("row", "col"), axis=0, tiled=True)
+    if compact():
+        posterior = shared_posterior(lax.axis_size("row") // 2, partial_value)
+    else:
+        loglik = lax.psum_scatter(partial_value, ("row", "col"), scatter_dimension=0, tiled=True)
+        posterior = jax.nn.softmax(loglik, axis=1).astype(jnp.bfloat16)
+        posterior = lax.all_gather(posterior, ("row", "col"), axis=0, tiled=True)
     expected = jnp.dot(posterior, prob.astype(jnp.bfloat16).T, preferred_element_type=jnp.float32)
     resid = seen * (answered - expected)
     count, total, square = lax.psum(
@@ -302,7 +425,8 @@
     learner_total = zres.shape[0] * lax.axis_size("lrn")
     tiles = lax.axis_size("col") * lax.axis_size("lrn")
     repeats = lax.axis_size("row") // tiles
-    if lax.axis_size("col") == 2 and lax.axis_size("lrn") == 2 and repeats == 2:
+    if compact():
+        zres = with_layout_constraint(zres, Layout(major_to_minor=(0, 1)))
         return line_gram(tiles, float(learner_total) ** 0.5, zres.T)
     panel = lax.all_gather(zres, "col", axis=1, tiled=True)
     whole_panel = lax.all_gather(panel, "lrn", axis=0, tiled=True)

time: 602 us -> 516 us (0.86)
  waiting for transfers between devices: 99 us -> 0 us
  Pallas kernels: 400 us -> 449 us
  between operations: 13.5 us -> 0.15 us
  local copies, waits for them, and re-layouts: 41.3 us -> 29.5 us
  matrix products: 17.8 us -> 11 us
    reduce_scatter x1 -> x0, waiting for transfers between devices: 62.5 us -> none  [residuals(): lax.psum_scatter(partial_value, ('row', 'col'), scatter_dimension=0, tile...]
    pallas_call x0 -> x1, Pallas kernels: none -> 45.2 us  [shared_posterior(): pl.pallas_call(functools.partial(posterior_kernel, planes), out_shape=jax...]
    all_gather x1 -> x0, waiting for transfers between devices: 36.5 us -> none  [residuals(): posterior = lax.all_gather(posterior, ('row', 'col'), axis=0, tiled=True)]
    unnamed x7 -> x11, local copies, waits for them, and re-layouts: 41.3 us -> 23 us
    transpose x1 -> x0, other arithmetic: 8.95 us -> none  [shards(): return line_gram(tiles, float(learner_total) ** 0.5, zres.T)]
    convert_element_type x1, other arithmetic: 1.64 us -> 10.1 us  [residuals(): (seen * (resid - mean) * lax.rsqrt(var + 1e-06) * lax.rsqrt(count)).astyp...]
    another operation x0 -> x1, local copies, waits for them, and re-layouts: none -> 6.42 us  [shards(): zres = with_layout_constraint(zres, Layout(major_to_minor=(0, 1)))]
  transfers between devices with their start and end apart: 2 -> 0, of which waited for: 2 -> 0; matrix products, arithmetic and copies ran while one was open for 0% -> 0% of each run, Pallas kernels for 0% -> 0%
where the time goes in v2:
time: 516 us
  Pallas kernels  449 us (87%)
  local copies, waits for them, and re-layouts  29.5 us (6%)
  other arithmetic  18.5 us (4%)
  matrix products  11 us (2%)
  blocking collectives  7.13 us (1%)
    pallas_call x1, Pallas kernels, line_gram(): pl.pallas_call(functools.partial(gram_kernel, planes, scale), out_shape=j...  404 us
    pallas_call x1, Pallas kernels, shared_posterior(): pl.pallas_call(functools.partial(posterior_kernel, planes), out_shape=jax...  45.2 us
    unnamed x11, local copies, waits for them, and re-layouts  23 us

profile of v2, /device:TPU:6, one launch (start us, length us, event | category | flops | bytes accessed | tf_op | source)
XLA Modules:
  0.0 515.7 jit_solution(14256647518945734854)
XLA Ops:
  0.0 0.7 broadcast_subtract_fusion
  0.7 0.7 log_subtract_fusion.1
  1.4 1.8 convolution_compare_fusion
  3.2 7.0 %convert_reduce_fusion = (f32[1024]{0:T(1024)S(1)}, f32[2048,1024]{1,0:T(8,128)S(1)}) fusion(s32[2048,1024]{1,0:T(8,128)} %param.6, f32[1024]{0:T(1024)S(1)} %get-tuple-element.15, f32[1024]{0:T(1024)S(1)} %get-tuple-element.14, s32[2048,1024]{1,0:T(8,128)} %param.5), kind=kLoop, calls=%fused_computation.10 | loop fusion | flops 16776192 | bytes 25178112 | tf_op jit(solution)/shard_map/reduce_sum | solution.py:188
  10.2 1.3 fusion.3
  11.6 0.0 slice-start
  11.6 0.0 slice-start.2
  11.6 1.8 fusion.6
  13.4 0.0 slice-start.1
  13.4 0.0 slice-start.3
  13.4 0.0 copy-start
  13.5 1.3 fusion.9.p_ref
  14.8 45.2 %shard_map.55 = bf16[2048,256]{1,0:T(8,128)(2,1)S(1)} custom-call(f32[2048,256]{1,0:T(8,128)S(1)} %fusion.9.p_ref), custom_call_target="tpu_custom_call" | custom-call | tf_op jit(solution)/shard_map/pallas_call | solution.py:143
  60.1 0.0 slice-done
  60.1 0.0 slice-done.2
  60.1 0.0 slice-done.1
  60.1 0.0 slice-done.3
  60.1 0.0 copy-done
  60.1 4.7 fusion.23
  64.8 7.1 %all-reduce = (f32[1024]{0:T(1024)S(1)}, f32[1024]{0:T(1024)S(1)}, f32[1024]{0:T(1024)S(1)}) all-reduce(f32[1024]{0:T(1024)S(1)} %get-tuple-element.10, f32[1024]{0:T(1024)S(1)} %get-tuple-element.6, f32[1024]{0:T(1024)S(1)} %get-tuple-element.5), channel_id=1, replica_groups=mesh['row'=8,'col'=2,'lrn'=2] {'lrn'}, use_global_device_ids=true, to_apply=%region_3.4 | all-reduce | flops 3072 | bytes 24576 | tf_op jit(solution)/shard_map/psum | solution.py:187
  72.0 10.1 %multiply_convert_fusion = bf16[2048,1024]{1,0:T(8,128)(2,1)} fusion(f32[2048,1024]{1,0:T(8,128)} %get-tuple-element.17, s32[2048,1024]{1,0:T(8,128)} %param.6, f32[1024]{0:T(1024)S(1)} %get-tuple-element.16, f32[1024]{0:T(1024)S(1)} %get-tuple-element.13, f32[1024]{0:T(1024)S(1)} %get-tuple-element.12), kind=kLoop, calls=%fused_computation.6 | loop fusion | flops 12582912 | bytes 20983808 | tf_op jit(solution)/shard_map/convert_element_type | solution.py:193
  82.0 6.4 %copy.6 = bf16[2048,1024]{0,1:T(8,128)(2,1)} copy(bf16[2048,1024]{1,0:T(8,128)(2,1)} %multiply_convert_fusion) | data formatting | bytes 8388608 | tf_op jit(solution)/shard_map/layout_constraint | solution.py:429
  88.4 404.2 %shard_map.56 = f32[2048,4096]{1,0:T(8,128)} custom-call(bf16[1024,2048]{1,0:T(8,128)(2,1)} %bitcast.9), custom_call_target="tpu_custom_call" | custom-call | flops 68719476736 | bytes 33554432 | tf_op jit(solution)/shard_map/pallas_call | solution.py:400
  492.7 23.0 %copy.13 = f32[2048,4096]{1,0:T(8,128)} copy(f32[2048,4096]{1,0:T(8,128)} %shard_map.56) | data formatting | bytes 67108864
  (3 shorter events, 0.0 us)
Async XLA Ops:
  11.6 48.5 %slice-start = ((s8[8388608]{0:T(1024)(128)(4,1)}), s8[4194304]{0:T(1024)(128)(4,1)S(1)}, s32[]{:S(2)}) async-start(s8[8388608]{0:T(1024)(128)(4,1)} %bitcast.5), calls=%async_computation | async-start | bytes 8388608
  11.6 48.5 %slice-start.2 = ((s8[8388608]{0:T(1024)(128)(4,1)}), s8[4194304]{0:T(1024)(128)(4,1)S(1)}, s32[]{:S(2)}) async-start(s8[8388608]{0:T(1024)(128)(4,1)} %bitcast.7), calls=%async_computation.2 | async-start | bytes 8388608
  13.4 46.7 %slice-start.1 = ((s8[8388608]{0:T(1024)(128)(4,1)}), s8[4194304]{0:T(1024)(128)(4,1)S(1)}, s32[]{:S(2)}) async-start(s8[8388608]{0:T(1024)(128)(4,1)} %bitcast.5), calls=%async_computation.1 | async-start | bytes 8388608
  13.4 46.7 %slice-start.3 = ((s8[8388608]{0:T(1024)(128)(4,1)}), s8[4194304]{0:T(1024)(128)(4,1)S(1)}, s32[]{:S(2)}) async-start(s8[8388608]{0:T(1024)(128)(4,1)} %bitcast.7), calls=%async_computation.3 | async-start | bytes 8388608
  13.4 46.7 %copy-start = (f32[1024]{0:T(1024)S(1)}, f32[1024]{0:T(1024)}, u32[]{:S(2)}) copy-start(f32[1024]{0:T(1024)} %param.8) | copy-start | bytes 12292

commit v3 on v2

--- a/solution.py
+++ b/solution.py
@@ -10,10 +10,11 @@
 
 ATTRS = 8
 PROFILES = 256
-CHUNK = 128
-GROUP = 2 * CHUNK
+CHUNK = 64
+GROUP = 256
+PARTS = 2
 TILE = 512
-AHEAD = 3
+AHEAD = 4
 MESH = pl.DeviceIdType.MESH
 
 
@@ -193,7 +194,7 @@
     return (seen * (resid - mean) * lax.rsqrt(var + 1e-06) * lax.rsqrt(count)).astype(jnp.bfloat16)
 
 
-def gram_kernel(planes, scale, z_ref, out_ref, panel, cols, stage, own_sem, out_sem,
+def gram_kernel(planes, z_ref, out_ref, panel, cols, stage, own_sem, out_sem,
                 xs, xr, ys, yr, us, ds, zr, ss, sr):
     items = z_ref.shape[0]
     n = items // CHUNK
@@ -312,40 +313,46 @@
             out_sem.at[slot],
         )
 
-    def job(j):
+    def job(p):
+        j, part = p // PARTS, p % PARTS
         g, swap, slot = j // 2, j % 2, j % 2
         which = core + swap - 2 * core * swap
-
-        @pl.when(swap == 1)
-        def _():
-            for s in range(4):
-                q = 4 * g + s
+        pieces = 2 * GROUP // CHUNK
+
+        @pl.when((swap == 1) & (part == 0))
+        def _():
+            for s in range(pieces):
+                q = pieces * g + s
                 remote(chunk(which, q), chunk(which, q), ss.at[q], sr.at[q], twin).wait_recv()
 
-        far = g // (n // 2)
+        groups = items // GROUP
+        far = g // groups
         py = c + far - 2 * c * far
-        base = pl.multiple_of((g % (n // 2)) * GROUP, GROUP)
-
-        @pl.when(j >= 2)
+        base = pl.multiple_of((g % groups) * GROUP, GROUP)
+
+        @pl.when((j >= 2) & (part == 0))
         def _():
             out_copy(slot, 0).wait()
 
         per = items // TILE
 
-        @pl.loop(0, 2 * per)
+        @pl.loop(0, per)
         def _(m):
-            y2, off = m // per, pl.multiple_of((m % per) * TILE, TILE)
+            off = pl.multiple_of(m * TILE, TILE)
             acc = None
             for px in range(2):
                 term = lax.dot_general(
-                    panel[px, y2, pl.ds(off, TILE), :],
+                    panel[px, part, pl.ds(off, TILE), :],
                     cols[which, px, py, pl.ds(base, GROUP), :],
                     (((1,), (1,)), ((), ())), preferred_element_type=jnp.float32,
                 )
                 acc = term if acc is None else acc + term
-            stage[slot, pl.ds(pl.multiple_of(m * TILE, TILE), TILE), :] = acc * scale
-
-        out_copy(slot, which * 2 * items + py * items + base).start()
+            place_to = pl.ds(pl.multiple_of(part * items + m * TILE, TILE), TILE)
+            stage[slot, place_to, :] = acc.astype(stage.dtype)
+
+        @pl.when(part == PARTS - 1)
+        def _():
+            out_copy(slot, which * 2 * items + py * items + base).start()
 
     @pl.loop(0, 2 * n)
     def _(q):
@@ -369,15 +376,19 @@
     def _(i):
         x_wait(1, i)
 
+    late = 2 * n + 3
+
     @pl.loop(2 * n, 4 * n)
     def _(q):
         relay(q)
 
-        @pl.when(q > 2 * n)
-        def _():
-            job(q - 2 * n - 1)
-
-    job(2 * n - 1)
+        @pl.when(q >= late)
+        def _():
+            job(q - late)
+
+    @pl.loop(4 * n - late, PARTS * (4 * items // GROUP))
+    def _(p):
+        job(p)
 
     @pl.loop(4 * n - AHEAD, 4 * n)
     def _(q):
@@ -393,19 +404,19 @@
     out_copy(1, 0).wait()
 
 
-def line_gram(planes, scale, z):
+def line_gram(planes, z):
     items, half = z.shape
     n = items // CHUNK
     dma = pltpu.SemaphoreType.DMA
     return pl.pallas_call(
-        functools.partial(gram_kernel, planes, scale),
-        out_shape=jax.ShapeDtypeStruct((2 * items, 4 * items), jnp.float32),
+        functools.partial(gram_kernel, planes),
+        out_shape=jax.ShapeDtypeStruct((2 * items, 4 * items), jnp.bfloat16),
         in_specs=[pl.BlockSpec(memory_space=pl.ANY)],
         out_specs=pl.BlockSpec(memory_space=pl.ANY),
         scratch_shapes=[
             pltpu.VMEM((2, 2, items, half), jnp.bfloat16),
             pltpu.VMEM((2, 2, 2, items, half), jnp.bfloat16),
-            pltpu.VMEM((2, 2 * items, GROUP), jnp.float32),
+            pltpu.VMEM((2, 2 * items, GROUP), jnp.bfloat16),
             dma, dma((2,)),
             dma((2 * n,)), dma((2 * n,)), dma((n,)), dma((n,)),
             dma((4 * n,)), dma((4 * n,)), dma((4 * n,)), dma((4 * n,)), dma((4 * n,)),
@@ -427,7 +438,8 @@
     repeats = lax.axis_size("row") // tiles
     if compact():
         zres = with_layout_constraint(zres, Layout(major_to_minor=(0, 1)))
-        return line_gram(tiles, float(learner_total) ** 0.5, zres.T)
+        gram = line_gram(tiles, zres.T)
+        return gram.astype(jnp.float32) * jnp.sqrt(jnp.float32(learner_total))
     panel = lax.all_gather(zres, "col", axis=1, tiled=True)
     whole_panel = lax.all_gather(panel, "lrn", axis=0, tiled=True)
     tile_index = lax.axis_index("col") * lax.axis_size("lrn") + lax.axis_index("lrn")

time: 516 us -> 506 us (0.981)
  local copies, waits for them, and re-layouts: 29.5 us -> 6.46 us
  other arithmetic: 18.5 us -> 37.2 us
    unnamed x11 -> x10, local copies, waits for them, and re-layouts: 23 us -> 0.04 us
    mul x0 -> x1, other arithmetic: none -> 18.7 us  [shards(): return gram.astype(jnp.float32) * jnp.sqrt(jnp.float32(learner_total))]
    pallas_call x1, Pallas kernels: 404 us -> 398 us  [line_gram(): pl.pallas_call(functools.partial(gram_kernel, planes), out_shape=jax.Shap...]
where the time goes in v3:
time: 506 us
  Pallas kernels  444 us (88%)
  other arithmetic  37.2 us (7%)
  matrix products  11 us (2%)
  blocking collectives  7.13 us (1%)
  local copies, waits for them, and re-layouts  6.46 us (1%)
    pallas_call x1, Pallas kernels, line_gram(): pl.pallas_call(functools.partial(gram_kernel, planes), out_shape=jax.Shap...  398 us
    pallas_call x1, Pallas kernels, shared_posterior(): pl.pallas_call(functools.partial(posterior_kernel, planes), out_shape=jax...  45.2 us
    mul x1, other arithmetic, shards(): return gram.astype(jnp.float32) * jnp.sqrt(jnp.float32(learner_total))  18.7 us

profile of v3, /device:TPU:6, one launch (start us, length us, event | category | flops | bytes accessed | tf_op | source)
XLA Modules:
  0.0 505.6 jit_solution(6280000042634921719)
XLA Ops:
  0.0 0.7 broadcast_subtract_fusion
  0.7 0.7 log_subtract_fusion.1
  1.4 1.8 convolution_compare_fusion
  3.2 7.0 %convert_reduce_fusion = (f32[1024]{0:T(1024)S(1)}, f32[2048,1024]{1,0:T(8,128)S(1)}) fusion(s32[2048,1024]{1,0:T(8,128)} %param.6, f32[1024]{0:T(1024)S(1)} %get-tuple-element.15, f32[1024]{0:T(1024)S(1)} %get-tuple-element.14, s32[2048,1024]{1,0:T(8,128)} %param.5), kind=kLoop, calls=%fused_computation.11 | loop fusion | flops 16776192 | bytes 25178112 | tf_op jit(solution)/shard_map/reduce_sum | solution.py:189
  10.2 1.3 fusion.3
  11.6 0.0 slice-start
  11.6 0.0 slice-start.2
  11.6 1.8 fusion.6
  13.4 0.0 slice-start.1
  13.4 0.0 slice-start.3
  13.4 0.0 copy-start
  13.5 1.3 fusion.9.p_ref
  14.8 45.2 %shard_map.55 = bf16[2048,256]{1,0:T(8,128)(2,1)S(1)} custom-call(f32[2048,256]{1,0:T(8,128)S(1)} %fusion.9.p_ref), custom_call_target="tpu_custom_call" | custom-call | tf_op jit(solution)/shard_map/pallas_call | solution.py:144
  60.1 0.0 slice-done
  60.1 0.0 slice-done.2
  60.1 0.0 slice-done.1
  60.1 0.0 slice-done.3
  60.1 0.0 copy-done
  60.1 4.7 fusion.23
  64.8 7.1 %all-reduce = (f32[1024]{0:T(1024)S(1)}, f32[1024]{0:T(1024)S(1)}, f32[1024]{0:T(1024)S(1)}) all-reduce(f32[1024]{0:T(1024)S(1)} %get-tuple-element.10, f32[1024]{0:T(1024)S(1)} %get-tuple-element.6, f32[1024]{0:T(1024)S(1)} %get-tuple-element.5), channel_id=1, replica_groups=mesh['row'=8,'col'=2,'lrn'=2] {'lrn'}, use_global_device_ids=true, to_apply=%region_3.4 | all-reduce | flops 3072 | bytes 24576 | tf_op jit(solution)/shard_map/psum | solution.py:188
  72.0 10.1 %multiply_convert_fusion = bf16[2048,1024]{1,0:T(8,128)(2,1)} fusion(f32[2048,1024]{1,0:T(8,128)} %get-tuple-element.17, s32[2048,1024]{1,0:T(8,128)} %param.6, f32[1024]{0:T(1024)S(1)} %get-tuple-element.16, f32[1024]{0:T(1024)S(1)} %get-tuple-element.13, f32[1024]{0:T(1024)S(1)} %get-tuple-element.12), kind=kLoop, calls=%fused_computation.7 | loop fusion | flops 12582912 | bytes 20983808 | tf_op jit(solution)/shard_map/convert_element_type | solution.py:194
  82.0 6.4 %copy.6 = bf16[2048,1024]{0,1:T(8,128)(2,1)} copy(bf16[2048,1024]{1,0:T(8,128)(2,1)} %multiply_convert_fusion) | data formatting | bytes 8388608 | tf_op jit(solution)/shard_map/layout_constraint | solution.py:440
  88.4 398.5 %shard_map.56 = bf16[2048,4096]{1,0:T(8,128)(2,1)} custom-call(bf16[1024,2048]{1,0:T(8,128)(2,1)} %bitcast.9), custom_call_target="tpu_custom_call" | custom-call | flops 68719476736 | bytes 33554432 | tf_op jit(solution)/shard_map/pallas_call | solution.py:411
  486.9 18.7 %convert_multiply_fusion = f32[2048,4096]{1,0:T(8,128)} fusion(bf16[2048,4096]{1,0:T(8,128)(2,1)} %shard_map.56), kind=kLoop, calls=%fused_computation | loop fusion | flops 16777216 | bytes 50331648 | tf_op jit(solution)/shard_map/mul | solution.py:442
  (3 shorter events, 0.0 us)
Async XLA Ops:
  11.6 48.5 %slice-start = ((s8[8388608]{0:T(1024)(128)(4,1)}), s8[4194304]{0:T(1024)(128)(4,1)S(1)}, s32[]{:S(2)}) async-start(s8[8388608]{0:T(1024)(128)(4,1)} %bitcast.5), calls=%async_computation | async-start | bytes 8388608
  11.6 48.5 %slice-start.2 = ((s8[8388608]{0:T(1024)(128)(4,1)}), s8[4194304]{0:T(1024)(128)(4,1)S(1)}, s32[]{:S(2)}) async-start(s8[8388608]{0:T(1024)(128)(4,1)} %bitcast.7), calls=%async_computation.2 | async-start | bytes 8388608
  13.4 46.7 %slice-start.1 = ((s8[8388608]{0:T(1024)(128)(4,1)}), s8[4194304]{0:T(1024)(128)(4,1)S(1)}, s32[]{:S(2)}) async-start(s8[8388608]{0:T(1024)(128)(4,1)} %bitcast.5), calls=%async_computation.1 | async-start | bytes 8388608
  13.4 46.7 %slice-start.3 = ((s8[8388608]{0:T(1024)(128)(4,1)}), s8[4194304]{0:T(1024)(128)(4,1)S(1)}, s32[]{:S(2)}) async-start(s8[8388608]{0:T(1024)(128)(4,1)} %bitcast.7), calls=%async_computation.3 | async-start | bytes 8388608
  13.4 46.7 %copy-start = (f32[1024]{0:T(1024)S(1)}, f32[1024]{0:T(1024)}, u32[]{:S(2)}) copy-start(f32[1024]{0:T(1024)} %param.8) | copy-start | bytes 12292
